TPU v7x, 512 devices: a whole 4x4x16 slice. The times are simulated.
512 devices in a mesh: dp: 32 (over x, z_hi, core), tensor: 16 (over z_lo, y).
Axes of the slice: x: 4, y: 4, z: 16 (z_hi: 4, z_lo: 4; z = z_hi * 4 + z_lo), core: 2. Of those that a mesh axis runs over, the one named last changes fastest.
Arguments:
- prefill_states: bfloat16 [256, 2, 64, 128, 128], P('dp', None, 'tensor'), may hold values from -6 to 6
- prompt_slot: int32 [256], replicated, may hold values from 0 to 255, as said below
- sample_prompt: int32 [4096], P('dp'), may hold values from 0 to 255, as said below
- queries: bfloat16 [4096, 2, 2, 8192], P('dp', None, None, 'tensor'), may hold values from -2 to 2
- keys: bfloat16 [4096, 2, 2, 8192], P('dp', None, None, 'tensor'), may hold values from -3 to 3
- values: bfloat16 [4096, 2, 2, 8192], P('dp', None, None, 'tensor'), may hold values from -6 to 6
- gates: bfloat16 [4096, 2, 2, 8192], P('dp', None, None, 'tensor'), may hold values from -6 to 6
- norm_gain: float32 [2, 8192], P(None, 'tensor'), may hold values from 0.25 to 1.75
- decay_rate: float32 [2, 64], P(None, 'tensor'), may hold values from 0.01 to 1
Outputs:
- attended: float32 [4096, 2, 2, 8192], P('dp', None, None, 'tensor')
Inputs may be any that keep to these rules, and one draw needn't show every extreme that they name: `prompt_slot`: A permutation: each slot holds one prompt; slot s lies with dp group s // 8. `sample_prompt`: rows g * 128 to (g + 1) * 128 - 1 hold, for r = 0 to 3, exactly 4 rows of each prompt whose slot lies with group (g - r * 8) modulo 256 / 8, in any order.
All inputs are finite; a program needn't handle non-finite values.
Results may differ from a plain program's by a relative error of at most 0.0003.
Values may be sent and summed in bfloat16 or wider, within the bound.
A program may use at most 64 MiB of HBM per device.

v0:
```python
import jax
import jax.numpy as jnp
from jax import lax
from jax.sharding import PartitionSpec as P

HEADS = 64
HEAD_DIM = 128


def shifted(block, axis, distance):
    devices = range(lax.axis_size(axis))
    route = [((i - distance) % len(devices), i) for i in devices]
    return lax.ppermute(block, axis, route)


def copy_for_each(shard, axis):
    copies = jnp.broadcast_to(shard, (lax.axis_size(axis), *shard.shape))
    return lax.all_to_all(copies, axis, split_axis=0, concat_axis=0, tiled=True)


def taken_together(shard, axis):
    return copy_for_each(shard, axis).sum(axis=0)


def against(query_block, states):
    return jnp.einsum(
        "psjlhd,plhde->psjlhe", query_block, states, preferred_element_type=jnp.float32
    )


def local(
    prefill_states, prompt_slot, sample_prompt, queries, keys, values, gates, norm_gain, decay_rate
):
    group = lax.axis_index("dp")
    groups = lax.axis_size("dp")
    quarter = groups // 4
    owned = prefill_states.shape[0]
    rows = sample_prompt.shape[0]
    steps = queries.shape[1]
    layers = decay_rate.shape[0]
    local_heads = decay_rate.shape[1]
    width = queries.shape[3] // local_heads
    per_prompt = rows // (4 * owned)
    prompt_count = prompt_slot.shape[0]
    match = sample_prompt[:, None] == jnp.arange(prompt_count, dtype=jnp.int32)[None, :]
    slots = jnp.sum(jnp.where(match, prompt_slot[None, :], 0), axis=1)
    owner = slots // owned
    within = slots % owned
    reach = (group - owner) % groups // quarter
    candidate = reach * owned + within
    order = jnp.argsort(candidate * rows + jnp.arange(rows, dtype=jnp.int32))
    inverse = jnp.argsort(order)
    sorted_queries = queries[order].reshape(4, owned, per_prompt, steps, layers, local_heads, width)
    results = [against(sorted_queries[0], prefill_states)]
    for stride in range(1, 4):
        arrived = shifted(sorted_queries[stride], "dp", groups - stride * quarter)
        answer = against(arrived, prefill_states)
        results.append(shifted(answer, "dp", stride * quarter))
    products = jnp.stack(results)
    products = products.reshape(rows, steps, layers, local_heads, width)[inverse]
    retain = jnp.exp(-decay_rate)[None, :, :, None]
    shape = (rows, steps, layers, local_heads, width)
    query_all = queries.reshape(shape)
    key_all = keys.reshape(shape)
    value_all = values.reshape(shape)
    first_first = jnp.einsum(
        "slhd,slhd->slh", query_all[:, 0], key_all[:, 0], preferred_element_type=jnp.float32
    )[..., None]
    second_first = jnp.einsum(
        "slhd,slhd->slh", query_all[:, 1], key_all[:, 0], preferred_element_type=jnp.float32
    )[..., None]
    second_second = jnp.einsum(
        "slhd,slhd->slh", query_all[:, 1], key_all[:, 1], preferred_element_type=jnp.float32
    )[..., None]
    value_one = value_all[:, 0].astype(jnp.float32)
    value_two = value_all[:, 1].astype(jnp.float32)
    out_one = retain * products[:, 0] + first_first * value_one
    out_two = (
        retain * retain * products[:, 1]
        + retain * second_first * value_one
        + second_second * value_two
    )
    mixed = jnp.stack([out_one, out_two], axis=1).reshape(rows, steps, layers, local_heads * width)
    total = taken_together(jnp.sum(mixed * mixed, axis=-1), "tensor")
    scale = lax.rsqrt(total / (HEADS * HEAD_DIM) + 1e-05)
    return (
        mixed * scale[..., None] * norm_gain[None, None] * jax.nn.sigmoid(gates.astype(jnp.float32))
    )


def solution(mesh):
    return jax.shard_map(
        local,
        mesh=mesh,
        in_specs=(
            P("dp", None, "tensor", None, None),
            P(),
            P("dp"),
            P("dp", None, None, "tensor"),
            P("dp", None, None, "tensor"),
            P("dp", None, None, "tensor"),
            P("dp", None, None, "tensor"),
            P(None, "tensor"),
            P(None, "tensor"),
        ),
        out_specs=P("dp", None, None, "tensor"),
        check_vma=False,
    )
```

profile of v0, /device:TPU:128, one launch (start us, length us, event | category | flops | bytes accessed | tf_op | source)
XLA Modules:
  0.0 83.8 jit_solution(16119852142922286425)
XLA Ops:
  0.0 1.0 %select_reduce_fusion = s32[128]{0:T(128)S(1)} fusion(s32[256]{0:T(256)} %param.10, s32[128]{0:T(128)} %param.11), kind=kLoop, calls=%fused_computation.36 | loop fusion | flops 98176 | bytes 2048 | tf_op jit(solution)/shard_map/reduce_sum | solution.py:46
  1.1 2.5 %sort.31 = (s32[128]{0:T(128)}, s32[128]{0:T(128)S(1)}) sort(s32[128]{0:T(128)S(1)} %iota_add_fusion, s32[128]{0:T(128)S(1)} %iota.15), dimensions={0}, to_apply=%region_1.2 | sort | flops 896 | bytes 2048 | tf_op jit(solution)/shard_map/jit(argsort)/sort | solution.py:51
  3.6 2.7 %gather_fusion = bf16[128,2,2,512]{3,2,1,0:T(2,128)(2,1)S(1)} fusion(bf16[128,2,2,512]{3,2,1,0:T(2,128)(2,1)} %param.12, s32[1024]{0:T(1024)S(1)} %pad_clamp_fusion.1), kind=kCustom, calls=%fused_computation | custom fusion | bytes 1049088 | tf_op jit(solution)/shard_map/gather | solution.py:53
  6.3 1.0 %fusion.30 = (bf16[32,2,2,512]{3,2,1,0:T(2,128)(2,1)S(1)}, bf16[32,2,2,512]{3,2,1,0:T(2,128)(2,1)S(1)}, bf16[32,2,2,512]{3,2,1,0:T(2,128)(2,1)S(1)}, bf16[32,2,2,512]{3,2,1,0:T(2,128)(2,1)}) fusion(bf16[128,2,2,512]{3,2,1,0:T(2,128)(2,1)S(1)} %gather_fusion), kind=kLoop, calls=%fused_computation.61 | loop fusion | bytes 1048576 | tf_op jit(solution)/shard_map/slice | solution.py:54
  7.3 1.0 %reshape.75 = bf16[8,4,2,2,4,128]{5,4,3,2,1,0:T(4,128)(2,1)S(1)} reshape(bf16[32,2,2,512]{3,2,1,0:T(2,128)(2,1)} %get-tuple-element.17) | data formatting | bytes 262144 | tf_op jit(solution)/shard_map/squeeze | solution.py:56
  8.3 0.7 copy.57
  9.0 3.4 %collective-permute-start.4 = (bf16[8,4,2,2,4,128]{5,1,2,4,3,0:T(4,128)(2,1)}, bf16[8,4,2,2,4,128]{5,1,2,4,3,0:T(4,128)(2,1)}, u32[]{:S(2)}, u32[]{:S(2)}) collective-permute-start(bf16[8,4,2,2,4,128]{5,1,2,4,3,0:T(4,128)(2,1)} %copy.57), channel_id=1, source_target_pairs={{384,0},{400,16},{416,32},{432,48},{448,64},{464,80},{480,96},{496... | collective-permute-start | bytes 393224 | tf_op jit(solution)/shard_map/ppermute | solution.py:13
  12.5 0.7 copy.53
  13.2 3.6 %collective-permute-start = (bf16[8,4,2,2,4,128]{5,1,2,4,3,0:T(4,128)(2,1)}, bf16[8,4,2,2,4,128]{5,1,2,4,3,0:T(4,128)(2,1)}, u32[]{:S(2)}, u32[]{:S(2)}) collective-permute-start(bf16[8,4,2,2,4,128]{5,1,2,4,3,0:T(4,128)(2,1)} %copy.53), channel_id=1, source_target_pairs={{128,0},{144,16},{160,32},{176,48},{192,64},{208,80},{224,96},{240... | collective-permute-start | bytes 393224 | tf_op jit(solution)/shard_map/ppermute | solution.py:13
  17.0 0.7 copy.55
  17.7 3.7 %collective-permute-start.2 = (bf16[8,4,2,2,4,128]{5,1,2,4,3,0:T(4,128)(2,1)}, bf16[8,4,2,2,4,128]{5,1,2,4,3,0:T(4,128)(2,1)}, u32[]{:S(2)}, u32[]{:S(2)}) collective-permute-start(bf16[8,4,2,2,4,128]{5,1,2,4,3,0:T(4,128)(2,1)} %copy.55), channel_id=1, source_target_pairs={{256,0},{272,16},{288,32},{304,48},{320,64},{336,80},{352,96},{368... | collective-permute-start | bytes 393224 | tf_op jit(solution)/shard_map/ppermute | solution.py:13
  21.8 2.5 %sort.32 = (s32[128]{0:T(128)}, s32[128]{0:T(128)S(1)}) sort(s32[128]{0:T(128)S(1)} %get-tuple-element.7, s32[128]{0:T(128)S(1)} %iota.16), dimensions={0}, to_apply=%region_2.3 | sort | flops 896 | bytes 2048 | tf_op jit(solution)/shard_map/jit(argsort)/sort | solution.py:52
  24.4 1.4 %reshape.42 = bf16[128,2,2,4,128]{4,3,2,1,0:T(4,128)(2,1)S(1)} reshape(bf16[128,2,2,512]{3,2,1,0:T(2,128)(2,1)} %param.13) | data formatting | bytes 1048576 | tf_op jit(solution)/shard_map/reshape | solution.py:64
  25.8 0.7 fusion.8
  26.4 1.9 %fusion.23 = (f32[128,2,4]{2,1,0:T(2,128)}, f32[128,2,4]{2,1,0:T(2,128)}, f32[128,2,4]{2,1,0:T(2,128)}) fusion(bf16[128,2,2,4,128]{4,3,2,1,0:T(4,128)(2,1)S(1)} %reshape.41, bf16[128,2,2,4,128]{4,3,2,1,0:T(4,128)(2,1)S(1)} %reshape.42), kind=kLoop, calls=%fused_computation.26 | loop fusion | flops 1307648 | bytes 1060864 | tf_op jit(solution)/shard_map/slhd,slhd->slh/dot_general | solution.py:66
  28.4 1.6 %fusion.17 = f32[8,4,2,2,4,128]{5,1,2,4,3,0:T(4,128)S(1)} fusion(bf16[8,4,2,2,4,128]{5,1,2,4,3,0:T(4,128)(2,1)} %collective-permute-done.4, bf16[8,2,4,128,128]{4,3,2,1,0:T(8,128)(2,1)S(1)} %copy-done), kind=kOutput, calls=%fused_computation.13 | convolution fusion | flops 16777216 | bytes 2490368 | tf_op jit(solution)/shard_map/psjlhd,plhde->psjlhe/dot_general | solution.py:26
  29.9 3.2 %collective-permute-start.5 = (f32[8,4,2,2,4,128]{5,1,2,4,3,0:T(4,128)S(1)}, f32[8,4,2,2,4,128]{5,1,2,4,3,0:T(4,128)}, u32[]{:S(2)}, u32[]{:S(2)}) collective-permute-start(f32[8,4,2,2,4,128]{5,1,2,4,3,0:T(4,128)S(1)} %fusion.17), channel_id=1, source_target_pairs={{128,0},{144,16},{160,32},{176,48},{192,64},{208,80},{224,96},{240... | collective-permute-start | bytes 786440 | tf_op jit(solution)/shard_map/ppermute | solution.py:13
  33.1 2.3 %fusion.11 = f32[8,4,2,2,4,128]{5,1,2,4,3,0:T(4,128)} fusion(bf16[8,4,2,2,4,128]{5,1,2,4,3,0:T(4,128)(2,1)} %collective-permute-done, bf16[8,2,4,128,128]{4,3,2,1,0:T(8,128)(2,1)S(1)} %copy-done), kind=kOutput, calls=%fused_computation.11 | convolution fusion | flops 16777216 | bytes 2490368 | tf_op jit(solution)/shard_map/psjlhd,plhde->psjlhe/dot_general | solution.py:26
  35.4 2.9 %collective-permute-start.1 = (f32[8,4,2,2,4,128]{5,1,2,4,3,0:T(4,128)}, f32[8,4,2,2,4,128]{5,1,2,4,3,0:T(4,128)}, u32[]{:S(2)}, u32[]{:S(2)}) collective-permute-start(f32[8,4,2,2,4,128]{5,1,2,4,3,0:T(4,128)} %fusion.11), channel_id=1, source_target_pairs={{384,0},{400,16},{416,32},{432,48},{448,64},{464,80},{480,96},{496... | collective-permute-start | bytes 786440 | tf_op jit(solution)/shard_map/ppermute | solution.py:13
  38.3 2.3 %fusion.14 = f32[8,4,2,2,4,128]{5,1,2,4,3,0:T(4,128)} fusion(bf16[8,4,2,2,4,128]{5,1,2,4,3,0:T(4,128)(2,1)} %collective-permute-done.2, bf16[8,2,4,128,128]{4,3,2,1,0:T(8,128)(2,1)S(1)} %copy-done), kind=kOutput, calls=%fused_computation.12 | convolution fusion | flops 16777216 | bytes 2490368 | tf_op jit(solution)/shard_map/psjlhd,plhde->psjlhe/dot_general | solution.py:26
  40.6 3.6 %collective-permute-start.3 = (f32[8,4,2,2,4,128]{5,1,2,4,3,0:T(4,128)}, f32[8,4,2,2,4,128]{5,1,2,4,3,0:T(4,128)}, u32[]{:S(2)}, u32[]{:S(2)}) collective-permute-start(f32[8,4,2,2,4,128]{5,1,2,4,3,0:T(4,128)} %fusion.14), channel_id=1, source_target_pairs={{256,0},{272,16},{288,32},{304,48},{320,64},{336,80},{352,96},{368... | collective-permute-start | bytes 786440 | tf_op jit(solution)/shard_map/ppermute | solution.py:13
  44.3 1.1 %reshape.43 = bf16[128,2,2,4,128]{4,3,2,1,0:T(4,128)(2,1)} reshape(bf16[128,2,2,512]{3,2,1,0:T(2,128)(2,1)S(1)} %copy-done.2) | data formatting | bytes 1048576 | tf_op jit(solution)/shard_map/reshape | solution.py:65
  45.4 6.1 %collective-permute-done.1 = f32[8,4,2,2,4,128]{5,1,2,4,3,0:T(4,128)} collective-permute-done((f32[8,4,2,2,4,128]{5,1,2,4,3,0:T(4,128)}, f32[8,4,2,2,4,128]{5,1,2,4,3,0:T(4,128)}, u32[]{:S(2)}, u32[]{:S(2)}) %collective-permute-start.1) | collective-permute-done | bytes 262176 | tf_op jit(solution)/shard_map/ppermute | solution.py:13
  51.5 1.4 %pad_maximum_fusion = f32[4,8,4,2,2,4,128]{6,2,3,5,4,1,0:T(4,128)S(1)} fusion(f32[1,8,4,2,2,4,128]{6,2,3,5,4,1,0:T(4,128)} %bitcast.10, f32[1,8,4,2,2,4,128]{6,2,3,5,4,1,0:T(4,128)} %bitcast.8, f32[1,8,4,2,2,4,128]{6,2,3,5,4,1,0:T(4,128)} %bitcast.6, f32[1,8,4,2,2,4,128]{6,2,3,5,4,1,0:T(4,128)S(1)} %fusion.8), kind=kLoop, calls=%fused_computation.15 | loop fusion | flops 786432 | bytes 2097152 | tf_op jit(solution)/shard_map/stack | solution.py:59
  53.3 1.6 %copy.59 = f32[128,2,2,4,128]{4,3,2,1,0:T(4,128)} copy(f32[128,2,2,4,128]{4,0,3,2,1:T(8,128)S(1)} %bitcast.65) | data formatting | bytes 2097152 | tf_op jit(solution)/shard_map/reshape | solution.py:60
  54.9 2.4 %gather_fusion.1 = f32[128,2,2,4,128]{4,3,2,1,0:T(4,128)S(1)} fusion(f32[128,2,2,4,128]{4,3,2,1,0:T(4,128)} %copy.59, s32[1024]{0:T(1024)S(1)} %pad_clamp_fusion), kind=kCustom, calls=%fused_computation.1 | custom fusion | bytes 2097664 | tf_op jit(solution)/shard_map/gather | solution.py:60
  57.3 2.8 %fusion.20 = (f32[128,1,2,4,128]{4,3,2,1,0:T(4,128)}, f32[128,1,2,4,128]{4,3,2,1,0:T(4,128)}) fusion(f32[128,2,2,4,128]{4,3,2,1,0:T(4,128)S(1)} %gather_fusion.1, f32[128,2,4]{2,1,0:T(2,128)S(1)} %copy-done.3, f32[2,4]{1,0:T(2,128)S(1)} %get-tuple-element.19, bf16[128,2,2,4,128]{4,3,2,1,0:T(4,128)(2,1)} %reshape.43, f32[128,2,4]{2,1,0:T(2,128)S(1)} %copy-done.4, ...), kind=kLoop, calls=%fused_computation.23 | loop fusion | flops 1310720 | bytes 2633792 | tf_op jit(solution)/shard_map/add | solution.py:77
  60.1 1.4 %stack.29 = f32[128,1,2,512]{3,2,0,1:T(2,128)S(1)} reshape(f32[128,1,2,4,128]{4,3,2,1,0:T(4,128)} %get-tuple-element.12) | data formatting | bytes 1048576 | tf_op jit(solution)/shard_map/stack | solution.py:83
  61.6 1.4 %stack.30 = f32[128,1,2,512]{3,2,0,1:T(2,128)S(1)} reshape(f32[128,1,2,4,128]{4,3,2,1,0:T(4,128)} %get-tuple-element.13) | data formatting | bytes 1048576 | tf_op jit(solution)/shard_map/stack | solution.py:83
  63.0 0.8 multiply_reduce_fusion
  63.9 16.6 %all_to_all.5 = f32[16,128,2,2]{1,3,2,0:T(2,128)S(1)} all-to-all(f32[16,128,2,2]{1,3,2,0:T(2,128)S(1)} %broadcast_in_dim.34), channel_id=1, replica_groups=mesh['dp'=32,'tensor'=16] {'tensor'}, dimensions={0} | all-to-all | bytes 65536 | tf_op jit(solution)/shard_map/all_to_all | solution.py:18
  80.7 3.1 %divide_multiply_fusion = f32[128,2,2,512]{3,2,1,0:T(2,128)} fusion(bf16[128,2,2,512]{3,2,1,0:T(2,128)(2,1)} %param.15, f32[2,512]{1,0:T(2,128)S(1)} %copy-done.6, f32[128,2,2]{2,1,0:T(2,128)S(1)} %copy.63, f32[128,1,2,512]{3,2,1,0:T(2,128)S(1)} %bitcast.64, f32[128,1,2,512]{3,2,1,0:T(2,128)S(1)} %bitcast.62), kind=kLoop, calls=%fused_computation.14 | loop fusion | flops 2097152 | bytes 2627584 | tf_op jit(solution)/shard_map/mul | solution.py:87
  (41 shorter events, 1.3 us)
Async XLA Ops:
  0.0 25.8 %copy-start = (bf16[8,2,4,128,128]{4,3,2,1,0:T(8,128)(2,1)S(1)}, bf16[8,2,4,128,128]{4,3,2,1,0:T(8,128)(2,1)}, u32[]{:S(2)}) copy-start(bf16[8,2,4,128,128]{4,3,2,1,0:T(8,128)(2,1)} %param.9) | copy-start | bytes 6291460
  0.0 21.4 %copy-start.1 = (bf16[128,2,2,512]{3,2,1,0:T(2,128)(2,1)S(1)}, bf16[128,2,2,512]{3,2,1,0:T(2,128)(2,1)}, u32[]{:S(2)}) copy-start(bf16[128,2,2,512]{3,2,1,0:T(2,128)(2,1)} %param.12) | copy-start | bytes 1572868
  7.3 18.4 %copy-start.7 = (f32[2,4]{1,0:T(2,128)S(1)}, f32[2,4]{1,0:T(2,128)}, u32[]{:S(2)}) copy-start(f32[2,4]{1,0:T(2,128)} %param.17) | copy-start | bytes 100
  9.0 19.4 %collective-permute-start.4 = (bf16[8,4,2,2,4,128]{5,1,2,4,3,0:T(4,128)(2,1)}, bf16[8,4,2,2,4,128]{5,1,2,4,3,0:T(4,128)(2,1)}, u32[]{:S(2)}, u32[]{:S(2)}) collective-permute-start(bf16[8,4,2,2,4,128]{5,1,2,4,3,0:T(4,128)(2,1)} %copy.57), channel_id=1, source_target_pairs={{384,0},{400,16},{416,32},{432,48},{448,64},{464,80},{480,96},{496... | collective-permute-start | bytes 393224 | tf_op jit(solution)/shard_map/ppermute | solution.py:13
  13.2 19.9 %collective-permute-start = (bf16[8,4,2,2,4,128]{5,1,2,4,3,0:T(4,128)(2,1)}, bf16[8,4,2,2,4,128]{5,1,2,4,3,0:T(4,128)(2,1)}, u32[]{:S(2)}, u32[]{:S(2)}) collective-permute-start(bf16[8,4,2,2,4,128]{5,1,2,4,3,0:T(4,128)(2,1)} %copy.53), channel_id=1, source_target_pairs={{128,0},{144,16},{160,32},{176,48},{192,64},{208,80},{224,96},{240... | collective-permute-start | bytes 393224 | tf_op jit(solution)/shard_map/ppermute | solution.py:13
  17.7 20.7 %collective-permute-start.2 = (bf16[8,4,2,2,4,128]{5,1,2,4,3,0:T(4,128)(2,1)}, bf16[8,4,2,2,4,128]{5,1,2,4,3,0:T(4,128)(2,1)}, u32[]{:S(2)}, u32[]{:S(2)}) collective-permute-start(bf16[8,4,2,2,4,128]{5,1,2,4,3,0:T(4,128)(2,1)} %copy.55), channel_id=1, source_target_pairs={{256,0},{272,16},{288,32},{304,48},{320,64},{336,80},{352,96},{368... | collective-permute-start | bytes 393224 | tf_op jit(solution)/shard_map/ppermute | solution.py:13
  29.9 14.3 %copy-start.2 = (bf16[128,2,2,512]{3,2,1,0:T(2,128)(2,1)S(1)}, bf16[128,2,2,512]{3,2,1,0:T(2,128)(2,1)}, u32[]{:S(2)}) copy-start(bf16[128,2,2,512]{3,2,1,0:T(2,128)(2,1)} %param.14) | copy-start | bytes 1572868
  29.9 15.5 %collective-permute-start.5 = (f32[8,4,2,2,4,128]{5,1,2,4,3,0:T(4,128)S(1)}, f32[8,4,2,2,4,128]{5,1,2,4,3,0:T(4,128)}, u32[]{:S(2)}, u32[]{:S(2)}) collective-permute-start(f32[8,4,2,2,4,128]{5,1,2,4,3,0:T(4,128)S(1)} %fusion.17), channel_id=1, source_target_pairs={{128,0},{144,16},{160,32},{176,48},{192,64},{208,80},{224,96},{240... | collective-permute-start | bytes 786440 | tf_op jit(solution)/shard_map/ppermute | solution.py:13
  35.4 10.0 %copy-start.5 = (f32[128,2,4]{2,1,0:T(2,128)S(1)}, f32[128,2,4]{2,1,0:T(2,128)}, u32[]{:S(2)}) copy-start(f32[128,2,4]{2,1,0:T(2,128)} %get-tuple-element.11) | copy-start | bytes 12292
  35.4 16.1 %collective-permute-start.1 = (f32[8,4,2,2,4,128]{5,1,2,4,3,0:T(4,128)}, f32[8,4,2,2,4,128]{5,1,2,4,3,0:T(4,128)}, u32[]{:S(2)}, u32[]{:S(2)}) collective-permute-start(f32[8,4,2,2,4,128]{5,1,2,4,3,0:T(4,128)} %fusion.11), channel_id=1, source_target_pairs={{384,0},{400,16},{416,32},{432,48},{448,64},{464,80},{480,96},{496... | collective-permute-start | bytes 786440 | tf_op jit(solution)/shard_map/ppermute | solution.py:13
  40.6 10.9 %collective-permute-start.3 = (f32[8,4,2,2,4,128]{5,1,2,4,3,0:T(4,128)}, f32[8,4,2,2,4,128]{5,1,2,4,3,0:T(4,128)}, u32[]{:S(2)}, u32[]{:S(2)}) collective-permute-start(f32[8,4,2,2,4,128]{5,1,2,4,3,0:T(4,128)} %fusion.14), channel_id=1, source_target_pairs={{256,0},{272,16},{288,32},{304,48},{320,64},{336,80},{352,96},{368... | collective-permute-start | bytes 786440 | tf_op jit(solution)/shard_map/ppermute | solution.py:13
  53.2 4.1 %copy-start.3 = (f32[128,2,4]{2,1,0:T(2,128)S(1)}, f32[128,2,4]{2,1,0:T(2,128)}, u32[]{:S(2)}) copy-start(f32[128,2,4]{2,1,0:T(2,128)} %get-tuple-element.9) | copy-start | bytes 12292
  53.2 4.1 %copy-start.4 = (f32[128,2,4]{2,1,0:T(2,128)S(1)}, f32[128,2,4]{2,1,0:T(2,128)}, u32[]{:S(2)}) copy-start(f32[128,2,4]{2,1,0:T(2,128)} %get-tuple-element.10) | copy-start | bytes 12292
  60.1 20.6 %copy-start.6 = (f32[2,512]{1,0:T(2,128)S(1)}, f32[2,512]{1,0:T(2,128)}, u32[]{:S(2)}) copy-start(f32[2,512]{1,0:T(2,128)} %param.16) | copy-start | bytes 12292
where the time goes:
time: 84.4 us; the launch traced here: 83.8 us
  starting transfers between devices  20.5 us (24%)
  local copies, waits for them, and re-layouts  17.4 us (21%)
  blocking collectives  16.6 us (20%)
  other arithmetic  16.2 us (19%)
  matrix products  6.74 us (8%)
  waiting for transfers between devices  6.1 us (7%)
    ppermute x6, starting transfers between devices, shifted(): return lax.ppermute(block, axis, route)  20.5 us
    all_to_all x1, blocking collectives, copy_for_each(): return lax.all_to_all(copies, axis, split_axis=0, concat_axis=0, tiled=True)  16.6 us
    dot_general x4, matrix products, against(): jnp.einsum('psjlhd,plhde->psjlhe', query_block, states, preferred_element...  6.74 us
    ppermute x6, waiting for transfers between devices, shifted(): return lax.ppermute(block, axis, route)  6.1 us
    squeeze x6, local copies, waits for them, and re-layouts, local(): arrived = shifted(sorted_queries[stride], 'dp', groups - stride * quarter)  3.29 us
    mul x1, other arithmetic, local(): mixed * scale[..., None] * norm_gain[None, None]  3.07 us
    another operation x2, local copies, waits for them, and re-layouts, local(): jnp.stack([out_one, out_two], axis=1)  2.88 us
    add x1, other arithmetic, local(): out_one = retain * products[:, 0] + first_first * value_one  2.77 us
  transfers between devices with their start and end apart: 6, of which 1 were waited for; matrix products, arithmetic and copies ran while one was open for 19% of the time, Pallas kernels for 0%

commit v1 on v0

v1 whole, which is shorter than its diff:
```python
import functools

import jax
import jax.numpy as jnp
from jax import lax
from jax.experimental import pallas as pl
from jax.experimental.pallas import tpu as pltpu
from jax.sharding import PartitionSpec as P

STEPS = 2
LAYERS = 2
READERS = 4
CHUNKS = 2
LANES = 128
TOP = 32767.0
FINE = 256.0
MESH = pl.DeviceIdType.MESH
F32, BF16, I32, I16 = jnp.float32, jnp.bfloat16, jnp.int32, jnp.int16


def iota(shape, axis):
    return lax.broadcasted_iota(I32, shape, axis)


def places(group, groups, owned, copies, sample_prompt, prompt_slot):
    prompts, rows = prompt_slot.shape[1], sample_prompt.shape[1]
    match = (iota((prompts, rows), 0) == sample_prompt).astype(F32).astype(BF16)
    slot_row = jnp.broadcast_to(prompt_slot.astype(F32), (8, prompts)).astype(BF16)
    slots = jnp.dot(slot_row, match, preferred_element_type=F32).astype(I32)[0:1]
    owner, within = slots // owned, slots % owned
    reach = ((group - owner + groups) % groups) // (groups // READERS)
    candidate = reach * owned + within
    count = READERS * owned
    mine = iota((count, rows), 0) == candidate
    earlier = (iota((rows, rows), 0) < iota((rows, rows), 1)).astype(F32).astype(BF16)
    before = jnp.dot(mine.astype(F32).astype(BF16), earlier, preferred_element_type=F32)
    rank = jnp.sum(jnp.where(mine, before, 0.0), axis=0, keepdims=True).astype(I32)
    place = jnp.clip(candidate * copies + rank, 0, rows - 1)
    at = (iota((rows, rows), 0) == place).astype(F32).astype(BF16)
    number = iota((8, rows), 1).astype(F32).astype(BF16)
    order = lax.dot_general(number, at, (((1,), (1,)), ((), ())), preferred_element_type=F32)
    order = jnp.clip(order.astype(I32), 0, rows - 1)
    return jnp.where(iota((8, rows), 0) == 0, order, jnp.broadcast_to(place, (8, rows)))


def kernel(
    groups,
    shards,
    states_hbm,
    slot_hbm,
    prompt_hbm,
    queries_hbm,
    keys_hbm,
    values_hbm,
    gates_hbm,
    gain_hbm,
    decay_ref,
    out_ref,
    states,
    slot_row,
    prompt_row,
    queries,
    rest,
    gain,
    index_vmem,
    index,
    sorted_q,
    arrived_q,
    spread_q,
    products,
    codes_out,
    codes_in,
    local_part,
    gated,
    mixed,
    squares,
    small_sem,
    big_sem,
    query_send,
    query_recv,
    code_send,
    code_recv,
    square_send,
    square_recv,
):
    group, shard = lax.axis_index("dp"), lax.axis_index("tensor")
    quarter = groups // READERS
    owned, layers, heads = states.shape[:3]
    rows, tile = queries.shape[:2]
    pairs = heads * layers
    block = rows // READERS
    part = block // CHUNKS
    copies = block // owned
    part_prompts = owned // CHUNKS

    def reader(r):
        return (lax.rem(group + quarter * r, groups), shard)

    others = [(group, lax.rem(shard + k, shards)) for k in range(1, shards)]

    first = [
        pltpu.make_async_copy(prompt_hbm, prompt_row, small_sem.at[0]),
        pltpu.make_async_copy(slot_hbm, slot_row, small_sem.at[1]),
    ]
    take_q = pltpu.make_async_copy(queries_hbm, queries, big_sem.at[0])
    take_states = pltpu.make_async_copy(states_hbm, states, big_sem.at[1])
    later = [
        pltpu.make_async_copy(ref, rest.at[n], big_sem.at[2 + n])
        for n, ref in enumerate((keys_hbm, values_hbm, gates_hbm))
    ]
    take_gain = pltpu.make_async_copy(gain_hbm, gain, small_sem.at[2])
    for copy in (*first, take_q, take_states, *later, take_gain):
        copy.start()

    barrier = pltpu.get_barrier_semaphore()
    met = [reader(r) for r in range(1, READERS)] + others
    for device in met:
        pl.semaphore_signal(barrier, inc=1, device_id=device, device_id_type=MESH)

    for copy in first:
        copy.wait()
    index_vmem[...] = places(group, groups, owned, copies, prompt_row[...], slot_row[...])
    take_index = pltpu.make_async_copy(index_vmem, index, small_sem.at[0])
    take_index.start()
    take_index.wait()
    take_q.wait()

    def at_index(which, n):
        return jnp.clip(index[which, n], 0, rows - 1)

    def gather(start, count):
        def step(n, carry):
            sorted_q[start + n] = queries[at_index(0, start + n)]
            return carry

        lax.fori_loop(0, count, step, 0, unroll=8)

    def query_copy(r, c):
        return pltpu.make_async_remote_copy(
            src_ref=sorted_q.at[pl.ds(r * block + c * part, part)],
            dst_ref=arrived_q.at[r - 1, pl.ds(c * part, part)],
            send_sem=query_send,
            recv_sem=query_recv.at[r - 1, c],
            device_id=reader(READERS - r),
            device_id_type=MESH,
        )

    def code_copy(r, c):
        return pltpu.make_async_remote_copy(
            src_ref=codes_out.at[r - 1, c],
            dst_ref=codes_in.at[r - 1, c],
            send_sem=code_send,
            recv_sem=code_recv.at[r - 1, c],
            device_id=reader(r),
            device_id_type=MESH,
        )

    hops = (1, 3, 2)
    met_all = False
    for c in range(CHUNKS):
        for r in hops:
            gather(r * block + c * part, part)
            if not met_all:
                pl.semaphore_wait(barrier, len(met))
                met_all = True
            query_copy(r, c).start()
    gather(0, block)

    def multiply(blocks, c):
        size = copies * tile
        for n, ref in enumerate(blocks):
            wide = ref[...].astype(F32).reshape(part * tile, LANES)
            spread_q[n, pl.ds(0, part * tile)] = wide

        def step(p, carry):
            for pair in range(pairs):
                left = [
                    spread_q[n, pl.ds(p * size + pair, copies * STEPS, stride=pairs), :]
                    for n in range(len(blocks))
                ]
                left = jnp.concatenate(left, axis=0) if len(left) > 1 else left[0]
                state = states[c * part_prompts + p, pair % layers, pair // layers]
                answer = jnp.dot(left.astype(BF16), state, preferred_element_type=F32)
                for n in range(len(blocks)):
                    products[n, pl.ds(p * size + pair, copies * STEPS, stride=pairs), :] = answer[
                        n * copies * STEPS : (n + 1) * copies * STEPS
                    ]
            return carry

        lax.fori_loop(0, part_prompts, step, 0)

    lane = iota((tile, LANES), 1)

    def encode(n, r, c):
        def step(j, scales):
            here = products[n, pl.ds(pl.multiple_of(j * tile, tile), tile), :]
            most = jnp.maximum(jnp.max(jnp.abs(here), axis=1, keepdims=True), 1e-30)
            scale = jnp.ceil(jnp.log2(most) * FINE + 0.25)
            code = jnp.round(here * (jnp.exp2(scale * (-1.0 / FINE)) * TOP))
            codes_out[r - 1, c, j] = code.astype(I32).astype(I16)
            return jnp.where(lane == j, scale, scales)

        scales = lax.fori_loop(0, part, step, jnp.zeros((tile, LANES), F32), unroll=4)
        codes_out[r - 1, c, part] = scales.astype(I32).astype(I16)

    row = iota((pairs, LANES), 0)
    decay = jnp.zeros((pairs, LANES), F32)
    for pair in range(pairs):
        decay = jnp.where(row == pair, decay_ref[pair % layers, pair // layers], decay)
    retain = jnp.exp(-decay)
    kept = jnp.concatenate([retain, retain * retain], axis=0)

    def add_up(j, total, sums):
        mixed[j] = total
        square = jnp.sum(total * total, axis=1, keepdims=True)
        return jnp.where(lane == j, square, sums)

    for copy in later:
        copy.wait()
    take_gain.wait()

    def terms(j, carry):
        at = at_index(0, j)
        query = sorted_q[j].astype(F32)
        key, value, gate = (rest[n, at].astype(F32) for n in range(3))
        one, two = slice(0, pairs), slice(pairs, tile)
        first_first = jnp.sum(query[one] * key[one], axis=1, keepdims=True)
        second_first = jnp.sum(query[two] * key[one], axis=1, keepdims=True)
        second_second = jnp.sum(query[two] * key[two], axis=1, keepdims=True)
        local_part[j, one] = first_first * value[one]
        local_part[j, two] = (second_first * retain) * value[one] + second_second * value[two]
        gains = jnp.concatenate([gain[...], gain[...]], axis=0)
        gated[j] = gains * jax.nn.sigmoid(gate)
        return carry

    lax.fori_loop(0, rows, terms, 0, unroll=4)

    take_states.wait()
    sums = jnp.zeros((tile, LANES), F32)
    for c in range(CHUNKS):
        multiply([sorted_q.at[pl.ds(c * part, part)]], c)

        def own(j, sums):
            reach = products[0, pl.ds(pl.multiple_of(j * tile, tile), tile), :]
            at = c * part + j
            return add_up(at, kept * reach + local_part[at], sums)

        sums = lax.fori_loop(0, part, own, sums, unroll=4)

    for c in range(CHUNKS):
        for some in ((1, 3), (2,)):
            for r in some:
                query_copy(r, c).wait_recv()
            multiply([arrived_q.at[r - 1, pl.ds(c * part, part)] for r in some], c)
            for n, r in enumerate(some):
                encode(n, r, c)
                code_copy(r, c).start()

    for c in range(CHUNKS):
        for r in hops:
            code_copy(r, c).wait_recv()
            scales = jnp.exp2(codes_in[r - 1, c, part].astype(I32).astype(F32) * (1.0 / FINE))
            scales = scales * (1.0 / TOP) * kept

            def decode(j, sums):
                at = r * block + c * part + j
                scale = jnp.sum(jnp.where(lane == j, scales, 0.0), axis=1, keepdims=True)
                reach = codes_in[r - 1, c, j].astype(I32).astype(F32) * scale
                return add_up(at, reach + local_part[at], sums)

            sums = lax.fori_loop(0, part, decode, sums, unroll=4)

    total = []
    for t in range(STEPS):
        here = sums[t * pairs : (t + 1) * pairs]
        for n in (pairs // 2, pairs // 4):
            here = here + pltpu.roll(here, n, 0)
        total.append(here)
    late = (row // layers) % STEPS == 1
    squares[0] = jnp.where(late, total[1], total[0])
    sends = []
    for k, device in enumerate(others):
        copy = pltpu.make_async_remote_copy(
            src_ref=squares.at[0],
            dst_ref=squares.at[k + 1],
            send_sem=square_send,
            recv_sem=square_recv,
            device_id=device,
            device_id_type=MESH,
        )
        copy.start()
    all_but_one = squares.at[pl.ds(1, shards - 1)]
    pltpu.make_async_copy(all_but_one, all_but_one, square_recv).wait()
    whole = squares[0]
    for k in range(1, shards):
        whole = whole + squares[k]
    scale = lax.rsqrt(whole / (shards * heads * LANES) + 1e-05)
    other = pltpu.roll(scale, layers, 0)
    scale = jnp.concatenate([jnp.where(late, other, scale), jnp.where(late, scale, other)], axis=0)

    def finish(j, carry):
        norm = jnp.sum(jnp.where(lane == j, scale, 0.0), axis=1, keepdims=True)
        mixed[j] = mixed[j] * norm * gated[j]
        return carry

    lax.fori_loop(0, rows, finish, 0, unroll=4)

    def place_back(n, carry):
        out_ref[n] = mixed[at_index(1, n)]
        return carry

    lax.fori_loop(0, rows, place_back, 0, unroll=8)

    pltpu.make_async_copy(all_but_one, all_but_one, square_send).wait()
    pltpu.make_async_copy(arrived_q, arrived_q, query_send).wait()
    pltpu.make_async_copy(codes_in, codes_in, code_send).wait()


def tiles(array, rows, heads):
    array = array.reshape(rows, STEPS, LAYERS, heads, LANES).transpose(0, 1, 3, 2, 4)
    return array.reshape(rows, STEPS * heads * LAYERS, LANES)


def local(
    prefill_states, prompt_slot, sample_prompt, queries, keys, values, gates, norm_gain, decay_rate
):
    groups, shards = lax.axis_size("dp"), lax.axis_size("tensor")
    owned, layers, heads = prefill_states.shape[:3]
    rows = sample_prompt.shape[0]
    tile = STEPS * heads * layers
    block = rows // READERS
    part = block // CHUNKS
    prompts = prompt_slot.shape[0]
    gain = norm_gain.reshape(layers, heads, LANES).transpose(1, 0, 2).reshape(heads * layers, LANES)
    hbm = pl.BlockSpec(memory_space=pltpu.HBM)
    vmem = pltpu.VMEM
    dma = pltpu.SemaphoreType.DMA
    out = pl.pallas_call(
        functools.partial(kernel, groups, shards),
        out_shape=jax.ShapeDtypeStruct((rows, tile, LANES), F32),
        in_specs=[hbm] * 8 + [pl.BlockSpec(memory_space=pltpu.SMEM)],
        out_specs=pl.BlockSpec(memory_space=pltpu.VMEM),
        scratch_shapes=[
            vmem(prefill_states.shape, BF16),
            vmem((1, prompts), I32),
            vmem((1, rows), I32),
            vmem((rows, tile, LANES), BF16),
            vmem((3, rows, tile, LANES), BF16),
            vmem((heads * layers, LANES), F32),
            vmem((8, rows), I32),
            pltpu.SMEM((8, rows), I32),
            vmem((rows, tile, LANES), BF16),
            vmem((READERS - 1, block, tile, LANES), BF16),
            vmem((2, part * tile + heads * layers * LAYERS * STEPS * 2, LANES), F32),
            vmem((2, part * tile + heads * layers * LAYERS * STEPS * 2, LANES), F32),
            vmem((READERS - 1, CHUNKS, part + 1, tile, LANES), I16),
            vmem((READERS - 1, CHUNKS, part + 1, tile, LANES), I16),
            vmem((rows, tile, LANES), F32),
            vmem((rows, tile, LANES), F32),
            vmem((rows, tile, LANES), F32),
            vmem((shards, heads * layers, LANES), F32),
            dma((3,)),
            dma((5,)),
            dma,
            dma((READERS - 1, CHUNKS)),
            dma,
            dma((READERS - 1, CHUNKS)),
            dma,
            dma,
        ],
        compiler_params=pltpu.CompilerParams(
            collective_id=0, has_side_effects=True, vmem_limit_bytes=56 * 2**20
        ),
        cost_estimate=pl.CostEstimate(flops=2**26, bytes_accessed=5 * 2**20, transcendentals=2**19),
    )(
        prefill_states,
        prompt_slot.reshape(1, prompts),
        sample_prompt.reshape(1, rows),
        tiles(queries, rows, heads),
        tiles(keys, rows, heads),
        tiles(values, rows, heads),
        tiles(gates, rows, heads),
        gain,
        decay_rate,
    )
    out = out.reshape(rows, STEPS, heads, LAYERS, LANES).transpose(0, 1, 3, 2, 4)
    return out.reshape(rows, STEPS, LAYERS, heads * LANES)


def solution(mesh):
    return jax.shard_map(
        local,
        mesh=mesh,
        in_specs=(
            P("dp", None, "tensor", None, None),
            P(),
            P("dp"),
            P("dp", None, None, "tensor"),
            P("dp", None, None, "tensor"),
            P("dp", None, None, "tensor"),
            P("dp", None, None, "tensor"),
            P(None, "tensor"),
            P(None, "tensor"),
        ),
        out_specs=P("dp", None, None, "tensor"),
        check_vma=False,
    )
```

time: 84.4 us -> 37.6 us (0.45)
  Pallas kernels: 0 us -> 34.9 us
  starting transfers between devices: 20.5 us -> 0 us
  blocking collectives: 16.6 us -> 0 us
  other arithmetic: 16.2 us -> 0 us
  local copies, waits for them, and re-layouts: 17.4 us -> 2.55 us
  matrix products: 6.74 us -> 0 us
  waiting for transfers between devices: 6.1 us -> 0 us
    pallas_call x0 -> x1, Pallas kernels: none -> 34.9 us  [local(): pl.pallas_call(functools.partial(kernel, groups, shards), out_shape=jax.S...]
    ppermute x6 -> x0, starting transfers between devices: 20.5 us -> none  [shifted(): return lax.ppermute(block, axis, route)]
    all_to_all x1 -> x0, blocking collectives: 16.6 us -> none  [copy_for_each(): return lax.all_to_all(copies, axis, split_axis=0, concat_axis=0, tiled=True)]
    dot_general x4 -> x0, matrix products: 6.74 us -> none  [against(): jnp.einsum('psjlhd,plhde->psjlhe', query_block, states, preferred_element...]
    ppermute x6 -> x0, waiting for transfers between devices: 6.1 us -> none  [shifted(): return lax.ppermute(block, axis, route)]
    gather x2 -> x0, local copies, waits for them, and re-layouts: 5.09 us -> none  [the longest x1 2.68 us: local(): queries[order]]
    sort x2 -> x0, other arithmetic: 5.06 us -> none  [the longest x1 2.54 us: local(): order = jnp.argsort(candidate * rows + jnp.arange(rows, dtype=jnp.int32))]
    reshape x4 -> x0, local copies, waits for them, and re-layouts: 4.47 us -> none  [the longest x1 1.65 us: local(): products.reshape(rows, steps, layers, local_heads, width)[inverse]]
  transfers between devices with their start and end apart: 6 -> 0, of which waited for: 1 -> 0; matrix products, arithmetic and copies ran while one was open for 19% -> 0% of each run, Pallas kernels for 0% -> 0%
where the time goes in v1:
time: 37.6 us; the launch traced here: 37.5 us
  Pallas kernels  34.9 us (93%)
  local copies, waits for them, and re-layouts  2.55 us (7%)
    pallas_call x1, Pallas kernels, local(): pl.pallas_call(functools.partial(kernel, groups, shards), out_shape=jax.S...  34.9 us
    unnamed x1, local copies, waits for them, and re-layouts  2.55 us

profile of v1, /device:TPU:128, one launch (start us, length us, event | category | flops | bytes accessed | tf_op | source)
XLA Modules:
  0.0 37.5 jit_solution(18434000245843300501)
XLA Ops:
  0.0 34.9 %shard_map.91 = f32[128,16,128]{2,1,0:T(8,128)} custom-call(bf16[8,2,4,128,128]{4,3,2,1,0:T(8,128)(2,1)} %states_hbm.1, s32[1,256]{1,0:T(1,128)} %bitcast.38, s32[1,128]{1,0:T(1,128)} %bitcast.39, bf16[128,16,128]{2,1,0:T(8,128)(2,1)} %bitcast.33, bf16[128,16,128]{2,1,0:T(8,128)(2,1)} %bitcast.34, bf16[128,16,128]{2,1,0:T(8,128)(2,1)} %bitcast.35, ...), custom_call_target="tpu_custom_call" | custom-call | flops 67108864 | bytes 5242880 | tf_op jit(solution)/shard_map/pallas_call | solution.py:338
  34.9 2.6 %copy.17 = f32[128,2,2,512]{3,2,1,0:T(2,128)} copy(f32[128,2,2,512]{3,2,1,0:T(2,128)} %bitcast.32) | data formatting | bytes 2097152

commit v2 on v1

--- a/solution.py
+++ b/solution.py
@@ -14,6 +14,7 @@
 LANES = 128
 TOP = 32767.0
 FINE = 256.0
+BATCH = 4
 MESH = pl.DeviceIdType.MESH
 F32, BF16, I32, I16 = jnp.float32, jnp.bfloat16, jnp.int32, jnp.int16
 
@@ -54,7 +55,7 @@
     values_hbm,
     gates_hbm,
     gain_hbm,
-    decay_ref,
+    decay_hbm,
     out_ref,
     states,
     slot_row,
@@ -64,6 +65,7 @@
     gain,
     index_vmem,
     index,
+    decay_ref,
     sorted_q,
     arrived_q,
     spread_q,
@@ -109,7 +111,8 @@
         for n, ref in enumerate((keys_hbm, values_hbm, gates_hbm))
     ]
     take_gain = pltpu.make_async_copy(gain_hbm, gain, small_sem.at[2])
-    for copy in (*first, take_q, take_states, *later, take_gain):
+    take_decay = pltpu.make_async_copy(decay_hbm, decay_ref, small_sem.at[3])
+    for copy in (*first, take_q, take_states, *later, take_gain, take_decay):
         copy.start()
 
     barrier = pltpu.get_barrier_semaphore()
@@ -172,68 +175,101 @@
             wide = ref[...].astype(F32).reshape(part * tile, LANES)
             spread_q[n, pl.ds(0, part * tile)] = wide
 
-        def step(p, carry):
+        for p in range(part_prompts):
             for pair in range(pairs):
-                left = [
-                    spread_q[n, pl.ds(p * size + pair, copies * STEPS, stride=pairs), :]
-                    for n in range(len(blocks))
-                ]
+                some = pl.ds(p * size + pair, copies * STEPS, stride=pairs)
+                left = [spread_q[n, some, :] for n in range(len(blocks))]
                 left = jnp.concatenate(left, axis=0) if len(left) > 1 else left[0]
                 state = states[c * part_prompts + p, pair % layers, pair // layers]
                 answer = jnp.dot(left.astype(BF16), state, preferred_element_type=F32)
                 for n in range(len(blocks)):
-                    products[n, pl.ds(p * size + pair, copies * STEPS, stride=pairs), :] = answer[
-                        n * copies * STEPS : (n + 1) * copies * STEPS
-                    ]
-            return carry
-
-        lax.fori_loop(0, part_prompts, step, 0)
-
+                    products[n, some, :] = answer[n * copies * STEPS : (n + 1) * copies * STEPS]
+
+    height = BATCH * tile
     lane = iota((tile, LANES), 1)
+    skew = jnp.concatenate([lane - n for n in range(BATCH)], axis=0)
+    ones = jnp.ones((2 * LANES, LANES), F32).astype(BF16)
+
+    def row_sums(wide):
+        high = wide.astype(BF16)
+        low = (wide - high.astype(F32)).astype(BF16)
+        return jnp.dot(jnp.concatenate([high, low], axis=1), ones, preferred_element_type=F32)
+
+    def spread(columns, j):
+        many = jnp.concatenate([columns] * BATCH, axis=0)
+        return row_sums(jnp.where(skew == j, many, 0.0))
+
+    def over_tiles(wide):
+        return sum(wide[n * tile : (n + 1) * tile] for n in range(BATCH))
+
+    def batches(count, step, carry):
+        return lax.fori_loop(0, count // BATCH, lambda b, had: step(b * BATCH, had), carry, unroll=2)
+
+    def some_products(n, j):
+        return products[n, pl.ds(pl.multiple_of(j * tile, height), height), :]
 
     def encode(n, r, c):
         def step(j, scales):
-            here = products[n, pl.ds(pl.multiple_of(j * tile, tile), tile), :]
+            here = some_products(n, j)
             most = jnp.maximum(jnp.max(jnp.abs(here), axis=1, keepdims=True), 1e-30)
             scale = jnp.ceil(jnp.log2(most) * FINE + 0.25)
             code = jnp.round(here * (jnp.exp2(scale * (-1.0 / FINE)) * TOP))
-            codes_out[r - 1, c, j] = code.astype(I32).astype(I16)
-            return jnp.where(lane == j, scale, scales)
-
-        scales = lax.fori_loop(0, part, step, jnp.zeros((tile, LANES), F32), unroll=4)
+            code = code.astype(I32).astype(I16)
+            codes_out[r - 1, c, pl.ds(j, BATCH)] = code.reshape(BATCH, tile, LANES)
+            return scales + over_tiles(jnp.where(skew == j, scale, 0.0))
+
+        scales = batches(part, step, jnp.zeros((tile, LANES), F32))
         codes_out[r - 1, c, part] = scales.astype(I32).astype(I16)
 
+    take_decay.wait()
     row = iota((pairs, LANES), 0)
     decay = jnp.zeros((pairs, LANES), F32)
     for pair in range(pairs):
         decay = jnp.where(row == pair, decay_ref[pair % layers, pair // layers], decay)
     retain = jnp.exp(-decay)
     kept = jnp.concatenate([retain, retain * retain], axis=0)
-
-    def add_up(j, total, sums):
-        mixed[j] = total
-        square = jnp.sum(total * total, axis=1, keepdims=True)
-        return jnp.where(lane == j, square, sums)
+    retains = jnp.concatenate([retain] * BATCH, axis=0)
+    kept_batch = jnp.concatenate([kept] * BATCH, axis=0)
+
+    def add_up(j, reach, sums):
+        total = reach + local_part[pl.ds(j, BATCH)].reshape(height, LANES)
+        mixed[pl.ds(j, BATCH)] = total.reshape(BATCH, tile, LANES)
+        square = row_sums(total * total)
+        for n in range(BATCH):
+            here = square[n * tile : (n + 1) * tile]
+            sums = jnp.where(lane == at_index(0, j + n), here, sums)
+        return sums
 
     for copy in later:
         copy.wait()
     take_gain.wait()
 
     def terms(j, carry):
-        at = at_index(0, j)
-        query = sorted_q[j].astype(F32)
-        key, value, gate = (rest[n, at].astype(F32) for n in range(3))
-        one, two = slice(0, pairs), slice(pairs, tile)
-        first_first = jnp.sum(query[one] * key[one], axis=1, keepdims=True)
-        second_first = jnp.sum(query[two] * key[one], axis=1, keepdims=True)
-        second_second = jnp.sum(query[two] * key[two], axis=1, keepdims=True)
-        local_part[j, one] = first_first * value[one]
-        local_part[j, two] = (second_first * retain) * value[one] + second_second * value[two]
-        gains = jnp.concatenate([gain[...], gain[...]], axis=0)
-        gated[j] = gains * jax.nn.sigmoid(gate)
+        query = sorted_q[pl.ds(j, BATCH)].astype(F32)
+        key, value = (
+            jnp.stack([rest[m, at_index(0, j + n)] for n in range(BATCH)]).astype(F32)
+            for m in range(2)
+        )
+
+        def of(wide, t):
+            return wide[:, t * pairs : (t + 1) * pairs].reshape(BATCH * pairs, LANES)
+
+        key_one, value_one = of(key, 0), of(value, 0)
+        inner = jnp.concatenate(
+            [of(query, 0) * key_one, of(query, 1) * key_one, of(query, 1) * of(key, 1)], axis=0
+        )
+        inner = row_sums(inner).reshape(3, BATCH * pairs, LANES)
+        term_one = inner[0] * value_one
+        term_two = inner[1] * retains * value_one + inner[2] * of(value, 1)
+        shape = (BATCH, pairs, LANES)
+        local_part[pl.ds(j, BATCH), 0:pairs] = term_one.reshape(shape)
+        local_part[pl.ds(j, BATCH), pairs:tile] = term_two.reshape(shape)
+        gate = rest[2, pl.ds(j, BATCH)].astype(F32)
+        gated[pl.ds(j, BATCH)] = gains[None] * jax.nn.sigmoid(gate)
         return carry
 
-    lax.fori_loop(0, rows, terms, 0, unroll=4)
+    gains = jnp.concatenate([gain[...], gain[...]], axis=0)
+    batches(rows, terms, 0)
 
     take_states.wait()
     sums = jnp.zeros((tile, LANES), F32)
@@ -241,11 +277,9 @@
         multiply([sorted_q.at[pl.ds(c * part, part)]], c)
 
         def own(j, sums):
-            reach = products[0, pl.ds(pl.multiple_of(j * tile, tile), tile), :]
-            at = c * part + j
-            return add_up(at, kept * reach + local_part[at], sums)
-
-        sums = lax.fori_loop(0, part, own, sums, unroll=4)
+            return add_up(c * part + j, kept_batch * some_products(0, j), sums)
+
+        sums = batches(part, own, sums)
 
     for c in range(CHUNKS):
         for some in ((1, 3), (2,)):
@@ -263,12 +297,11 @@
             scales = scales * (1.0 / TOP) * kept
 
             def decode(j, sums):
-                at = r * block + c * part + j
-                scale = jnp.sum(jnp.where(lane == j, scales, 0.0), axis=1, keepdims=True)
-                reach = codes_in[r - 1, c, j].astype(I32).astype(F32) * scale
-                return add_up(at, reach + local_part[at], sums)
-
-            sums = lax.fori_loop(0, part, decode, sums, unroll=4)
+                code = codes_in[r - 1, c, pl.ds(j, BATCH)].astype(I32).astype(F32)
+                reach = code.reshape(height, LANES) * spread(scales, j)
+                return add_up(r * block + c * part + j, reach, sums)
+
+            sums = batches(part, decode, sums)
 
     total = []
     for t in range(STEPS):
@@ -299,17 +332,12 @@
     scale = jnp.concatenate([jnp.where(late, other, scale), jnp.where(late, scale, other)], axis=0)
 
     def finish(j, carry):
-        norm = jnp.sum(jnp.where(lane == j, scale, 0.0), axis=1, keepdims=True)
-        mixed[j] = mixed[j] * norm * gated[j]
+        here = jnp.stack([mixed[at_index(1, j + n)] for n in range(BATCH)])
+        norm = spread(scale, j).reshape(BATCH, tile, LANES)
+        out_ref[pl.ds(j, BATCH)] = here * norm * gated[pl.ds(j, BATCH)]
         return carry
 
-    lax.fori_loop(0, rows, finish, 0, unroll=4)
-
-    def place_back(n, carry):
-        out_ref[n] = mixed[at_index(1, n)]
-        return carry
-
-    lax.fori_loop(0, rows, place_back, 0, unroll=8)
+    batches(rows, finish, 0)
 
     pltpu.make_async_copy(all_but_one, all_but_one, square_send).wait()
     pltpu.make_async_copy(arrived_q, arrived_q, query_send).wait()
@@ -332,13 +360,13 @@
     part = block // CHUNKS
     prompts = prompt_slot.shape[0]
     gain = norm_gain.reshape(layers, heads, LANES).transpose(1, 0, 2).reshape(heads * layers, LANES)
-    hbm = pl.BlockSpec(memory_space=pltpu.HBM)
+    hbm = pl.BlockSpec(memory_space=pl.ANY)
     vmem = pltpu.VMEM
     dma = pltpu.SemaphoreType.DMA
     out = pl.pallas_call(
         functools.partial(kernel, groups, shards),
         out_shape=jax.ShapeDtypeStruct((rows, tile, LANES), F32),
-        in_specs=[hbm] * 8 + [pl.BlockSpec(memory_space=pltpu.SMEM)],
+        in_specs=[hbm] * 9,
         out_specs=pl.BlockSpec(memory_space=pltpu.VMEM),
         scratch_shapes=[
             vmem(prefill_states.shape, BF16),
@@ -349,6 +377,7 @@
             vmem((heads * layers, LANES), F32),
             vmem((8, rows), I32),
             pltpu.SMEM((8, rows), I32),
+            pltpu.SMEM(decay_rate.shape, F32),
             vmem((rows, tile, LANES), BF16),
             vmem((READERS - 1, block, tile, LANES), BF16),
             vmem((2, part * tile + heads * layers * LAYERS * STEPS * 2, LANES), F32),
@@ -359,7 +388,7 @@
             vmem((rows, tile, LANES), F32),
             vmem((rows, tile, LANES), F32),
             vmem((shards, heads * layers, LANES), F32),
-            dma((3,)),
+            dma((4,)),
             dma((5,)),
             dma,
             dma((READERS - 1, CHUNKS)),
@@ -369,19 +398,18 @@
             dma,
         ],
         compiler_params=pltpu.CompilerParams(
-            collective_id=0, has_side_effects=True, vmem_limit_bytes=56 * 2**20
+            collective_id=0, has_side_effects=True, vmem_limit_bytes=32 * 2**20
         ),
         cost_estimate=pl.CostEstimate(flops=2**26, bytes_accessed=5 * 2**20, transcendentals=2**19),
     )(
-        prefill_states,
+        *(pltpu.with_memory_space_constraint(x, pltpu.HBM) for x in (prefill_states,
         prompt_slot.reshape(1, prompts),
         sample_prompt.reshape(1, rows),
         tiles(queries, rows, heads),
         tiles(keys, rows, heads),
         tiles(values, rows, heads),
         tiles(gates, rows, heads),
-        gain,
-        decay_rate,
+        gain, decay_rate)),
     )
     out = out.reshape(rows, STEPS, heads, LAYERS, LANES).transpose(0, 1, 3, 2, 4)
     return out.reshape(rows, STEPS, LAYERS, heads * LANES)

time: 37.6 us -> 31.8 us (0.85)
  Pallas kernels: 34.9 us -> 30.7 us
  local copies, waits for them, and re-layouts: 2.55 us -> 0.97 us
    pallas_call x1, Pallas kernels: 34.9 us -> 30.7 us  [local(): pl.pallas_call(functools.partial(kernel, groups, shards), out_shape=jax.S...]
    unnamed x1, local copies, waits for them, and re-layouts: 2.55 us -> 0.97 us
where the time goes in v2:
time: 31.8 us; the launch traced here: 31.7 us
  Pallas kernels  30.7 us (97%)
  local copies, waits for them, and re-layouts  0.97 us (3%)
    pallas_call x1, Pallas kernels, local(): pl.pallas_call(functools.partial(kernel, groups, shards), out_shape=jax.S...  30.7 us
    unnamed x1, local copies, waits for them, and re-layouts  0.97 us

profile of v2, /device:TPU:128, one launch (start us, length us, event | category | flops | bytes accessed | tf_op | source)
XLA Modules:
  0.0 31.7 jit_solution(2448487377788358555)
XLA Ops:
  0.0 30.7 %shard_map.91 = f32[128,16,128]{2,1,0:T(8,128)S(1)} custom-call(bf16[8,2,4,128,128]{4,3,2,1,0:T(8,128)(2,1)} %states_hbm.1, s32[1,256]{1,0:T(1,128)} %bitcast.38, s32[1,128]{1,0:T(1,128)} %bitcast.39, bf16[128,16,128]{2,1,0:T(8,128)(2,1)} %bitcast.33, bf16[128,16,128]{2,1,0:T(8,128)(2,1)} %bitcast.34, bf16[128,16,128]{2,1,0:T(8,128)(2,1)} %bitcast.35, ...), custom_call_target="tpu_custom_call" | custom-call | flops 67108864 | bytes 5242880 | tf_op jit(solution)/shard_map/pallas_call | solution.py:366
  30.7 1.0 %copy.17 = f32[128,2,2,512]{3,2,1,0:T(2,128)} copy(f32[128,2,2,512]{3,2,1,0:T(2,128)S(1)} %bitcast.32) | data formatting | bytes 2097152

commit v3 on v2

--- a/solution.py
+++ b/solution.py
@@ -14,7 +14,7 @@
 LANES = 128
 TOP = 32767.0
 FINE = 256.0
-BATCH = 4
+BATCH = 16
 MESH = pl.DeviceIdType.MESH
 F32, BF16, I32, I16 = jnp.float32, jnp.bfloat16, jnp.int32, jnp.int16
 
@@ -189,21 +189,26 @@
     lane = iota((tile, LANES), 1)
     skew = jnp.concatenate([lane - n for n in range(BATCH)], axis=0)
     ones = jnp.ones((2 * LANES, LANES), F32).astype(BF16)
-
-    def row_sums(wide):
+    first_lanes = jnp.where(skew == 0, 1.0, 0.0).astype(BF16)
+    first_lanes = jnp.concatenate([first_lanes, first_lanes], axis=1)
+
+    def halves(wide):
         high = wide.astype(BF16)
         low = (wide - high.astype(F32)).astype(BF16)
-        return jnp.dot(jnp.concatenate([high, low], axis=1), ones, preferred_element_type=F32)
-
-    def spread(columns, j):
-        many = jnp.concatenate([columns] * BATCH, axis=0)
-        return row_sums(jnp.where(skew == j, many, 0.0))
+        return jnp.concatenate([high, low], axis=1)
+
+    def row_sums(wide):
+        return jnp.dot(halves(wide), ones, preferred_element_type=F32)
+
+    def spread(columns):
+        many = jnp.concatenate([halves(columns)] * BATCH, axis=0) * first_lanes
+        return jnp.dot(many, ones, preferred_element_type=F32)
 
     def over_tiles(wide):
         return sum(wide[n * tile : (n + 1) * tile] for n in range(BATCH))
 
     def batches(count, step, carry):
-        return lax.fori_loop(0, count // BATCH, lambda b, had: step(b * BATCH, had), carry, unroll=2)
+        return lax.fori_loop(0, count // BATCH, lambda b, had: step(b * BATCH, had), carry)
 
     def some_products(n, j):
         return products[n, pl.ds(pl.multiple_of(j * tile, height), height), :]
@@ -298,7 +303,7 @@
 
             def decode(j, sums):
                 code = codes_in[r - 1, c, pl.ds(j, BATCH)].astype(I32).astype(F32)
-                reach = code.reshape(height, LANES) * spread(scales, j)
+                reach = code.reshape(height, LANES) * spread(scales)
                 return add_up(r * block + c * part + j, reach, sums)
 
             sums = batches(part, decode, sums)
@@ -322,6 +327,13 @@
             device_id_type=MESH,
         )
         copy.start()
+
+    def gate_all(j, carry):
+        here = jnp.stack([mixed[at_index(1, j + n)] for n in range(BATCH)])
+        out_ref[pl.ds(j, BATCH)] = here * gated[pl.ds(j, BATCH)]
+        return carry
+
+    batches(rows, gate_all, 0)
     all_but_one = squares.at[pl.ds(1, shards - 1)]
     pltpu.make_async_copy(all_but_one, all_but_one, square_recv).wait()
     whole = squares[0]
@@ -331,13 +343,12 @@
     other = pltpu.roll(scale, layers, 0)
     scale = jnp.concatenate([jnp.where(late, other, scale), jnp.where(late, scale, other)], axis=0)
 
-    def finish(j, carry):
-        here = jnp.stack([mixed[at_index(1, j + n)] for n in range(BATCH)])
-        norm = spread(scale, j).reshape(BATCH, tile, LANES)
-        out_ref[pl.ds(j, BATCH)] = here * norm * gated[pl.ds(j, BATCH)]
-        return carry
-
-    batches(rows, finish, 0)
+    def finish(j, columns):
+        norm = spread(columns).reshape(BATCH, tile, LANES)
+        out_ref[pl.ds(j, BATCH)] = out_ref[pl.ds(j, BATCH)] * norm
+        return pltpu.roll(columns, LANES - BATCH, 1)
+
+    batches(rows, finish, scale)
 
     pltpu.make_async_copy(all_but_one, all_but_one, square_send).wait()
     pltpu.make_async_copy(arrived_q, arrived_q, query_send).wait()

time: 31.8 us -> 30.5 us (0.959)
  Pallas kernels: 30.7 us -> 29.4 us
    pallas_call x1, Pallas kernels: 30.7 us -> 29.4 us  [local(): pl.pallas_call(functools.partial(kernel, groups, shards), out_shape=jax.S...]
where the time goes in v3:
time: 30.5 us; the launch traced here: 30.4 us
  Pallas kernels  29.4 us (96%)
  local copies, waits for them, and re-layouts  0.97 us (3%)
    pallas_call x1, Pallas kernels, local(): pl.pallas_call(functools.partial(kernel, groups, shards), out_shape=jax.S...  29.4 us
    unnamed x1, local copies, waits for them, and re-layouts  0.97 us

profile of v3, /device:TPU:128, one launch (start us, length us, event | category | flops | bytes accessed | tf_op | source)
XLA Modules:
  0.0 30.4 jit_solution(4475693101989137278)
XLA Ops:
  0.0 29.4 %shard_map.91 = f32[128,16,128]{2,1,0:T(8,128)S(1)} custom-call(bf16[8,2,4,128,128]{4,3,2,1,0:T(8,128)(2,1)} %states_hbm.1, s32[1,256]{1,0:T(1,128)} %bitcast.38, s32[1,128]{1,0:T(1,128)} %bitcast.39, bf16[128,16,128]{2,1,0:T(8,128)(2,1)} %bitcast.33, bf16[128,16,128]{2,1,0:T(8,128)(2,1)} %bitcast.34, bf16[128,16,128]{2,1,0:T(8,128)(2,1)} %bitcast.35, ...), custom_call_target="tpu_custom_call" | custom-call | flops 67108864 | bytes 5242880 | tf_op jit(solution)/shard_map/pallas_call | solution.py:377
  29.4 1.0 %copy.17 = f32[128,2,2,512]{3,2,1,0:T(2,128)} copy(f32[128,2,2,512]{3,2,1,0:T(2,128)S(1)} %bitcast.32) | data formatting | bytes 2097152

commit v4 on v3

--- a/solution.py
+++ b/solution.py
@@ -23,13 +23,18 @@
     return lax.broadcasted_iota(I32, shape, axis)
 
 
+def bits(size):
+    assert size & (size - 1) == 0
+    return size.bit_length() - 1
+
+
 def places(group, groups, owned, copies, sample_prompt, prompt_slot):
     prompts, rows = prompt_slot.shape[1], sample_prompt.shape[1]
     match = (iota((prompts, rows), 0) == sample_prompt).astype(F32).astype(BF16)
     slot_row = jnp.broadcast_to(prompt_slot.astype(F32), (8, prompts)).astype(BF16)
     slots = jnp.dot(slot_row, match, preferred_element_type=F32).astype(I32)[0:1]
-    owner, within = slots // owned, slots % owned
-    reach = ((group - owner + groups) % groups) // (groups // READERS)
+    owner, within = slots >> bits(owned), slots & (owned - 1)
+    reach = ((group - owner + groups) & (groups - 1)) >> bits(groups // READERS)
     candidate = reach * owned + within
     count = READERS * owned
     mine = iota((count, rows), 0) == candidate
@@ -112,13 +117,16 @@
     ]
     take_gain = pltpu.make_async_copy(gain_hbm, gain, small_sem.at[2])
     take_decay = pltpu.make_async_copy(decay_hbm, decay_ref, small_sem.at[3])
-    for copy in (*first, take_q, take_states, *later, take_gain, take_decay):
+    for copy in first:
         copy.start()
-
     barrier = pltpu.get_barrier_semaphore()
     met = [reader(r) for r in range(1, READERS)] + others
-    for device in met:
+    for n, device in enumerate(met):
         pl.semaphore_signal(barrier, inc=1, device_id=device, device_id_type=MESH)
+        if n == READERS - 2:
+            take_q.start()
+    for copy in (take_states, *later, take_gain, take_decay):
+        copy.start()
 
     for copy in first:
         copy.wait()
@@ -158,7 +166,7 @@
             device_id_type=MESH,
         )
 
-    hops = (1, 3, 2)
+    hops = (2, 1, 3)
     met_all = False
     for c in range(CHUNKS):
         for r in hops:
@@ -287,7 +295,7 @@
         sums = batches(part, own, sums)
 
     for c in range(CHUNKS):
-        for some in ((1, 3), (2,)):
+        for some in ((2,), (1, 3)):
             for r in some:
                 query_copy(r, c).wait_recv()
             multiply([arrived_q.at[r - 1, pl.ds(c * part, part)] for r in some], c)
@@ -343,12 +351,9 @@
     other = pltpu.roll(scale, layers, 0)
     scale = jnp.concatenate([jnp.where(late, other, scale), jnp.where(late, scale, other)], axis=0)
 
-    def finish(j, columns):
-        norm = spread(columns).reshape(BATCH, tile, LANES)
-        out_ref[pl.ds(j, BATCH)] = out_ref[pl.ds(j, BATCH)] * norm
-        return pltpu.roll(columns, LANES - BATCH, 1)
-
-    batches(rows, finish, scale)
+    for j in range(0, rows, BATCH):
+        norm = spread(pltpu.roll(scale, LANES - j, 1) if j else scale)
+        out_ref[pl.ds(j, BATCH)] = out_ref[pl.ds(j, BATCH)] * norm.reshape(BATCH, tile, LANES)
 
     pltpu.make_async_copy(all_but_one, all_but_one, square_send).wait()
     pltpu.make_async_copy(arrived_q, arrived_q, query_send).wait()

time: 30.5 us -> 28.9 us (0.948)
  Pallas kernels: 29.4 us -> 27.8 us
    pallas_call x1, Pallas kernels: 29.4 us -> 27.8 us  [local(): pl.pallas_call(functools.partial(kernel, groups, shards), out_shape=jax.S...]
where the time goes in v4:
time: 28.9 us; the launch traced here: 28.8 us
  Pallas kernels  27.8 us (96%)
  local copies, waits for them, and re-layouts  0.97 us (3%)
    pallas_call x1, Pallas kernels, local(): pl.pallas_call(functools.partial(kernel, groups, shards), out_shape=jax.S...  27.8 us
    unnamed x1, local copies, waits for them, and re-layouts  0.97 us

profile of v4, /device:TPU:128, one launch (start us, length us, event | category | flops | bytes accessed | tf_op | source)
XLA Modules:
  0.0 28.8 jit_solution(7887065976199375175)
XLA Ops:
  0.0 27.8 %shard_map.91 = f32[128,16,128]{2,1,0:T(8,128)S(1)} custom-call(bf16[8,2,4,128,128]{4,3,2,1,0:T(8,128)(2,1)} %states_hbm.1, s32[1,256]{1,0:T(1,128)} %bitcast.38, s32[1,128]{1,0:T(1,128)} %bitcast.39, bf16[128,16,128]{2,1,0:T(8,128)(2,1)} %bitcast.33, bf16[128,16,128]{2,1,0:T(8,128)(2,1)} %bitcast.34, bf16[128,16,128]{2,1,0:T(8,128)(2,1)} %bitcast.35, ...), custom_call_target="tpu_custom_call" | custom-call | flops 67108864 | bytes 5242880 | tf_op jit(solution)/shard_map/pallas_call | solution.py:382
  27.8 1.0 %copy.17 = f32[128,2,2,512]{3,2,1,0:T(2,128)} copy(f32[128,2,2,512]{3,2,1,0:T(2,128)S(1)} %bitcast.32) | data formatting | bytes 2097152

commit v5 on v4

--- a/solution.py
+++ b/solution.py
@@ -101,9 +101,9 @@
     part_prompts = owned // CHUNKS
 
     def reader(r):
-        return (lax.rem(group + quarter * r, groups), shard)
-
-    others = [(group, lax.rem(shard + k, shards)) for k in range(1, shards)]
+        return ((group + quarter * r) & (groups - 1), shard)
+
+    others = [k + (shard <= k).astype(I32) for k in range(shards - 1)]
 
     first = [
         pltpu.make_async_copy(prompt_hbm, prompt_row, small_sem.at[0]),
@@ -120,7 +120,8 @@
     for copy in first:
         copy.start()
     barrier = pltpu.get_barrier_semaphore()
-    met = [reader(r) for r in range(1, READERS)] + others
+    met = [reader(r) for r in range(1, READERS)]
+    met += [(group, other) for other in others]
     for n, device in enumerate(met):
         pl.semaphore_signal(barrier, inc=1, device_id=device, device_id_type=MESH)
         if n == READERS - 2:
@@ -167,13 +168,13 @@
         )
 
     hops = (2, 1, 3)
-    met_all = False
+    for r in hops:
+        gather(r * block, part)
+    pl.semaphore_wait(barrier, len(met))
     for c in range(CHUNKS):
         for r in hops:
-            gather(r * block + c * part, part)
-            if not met_all:
-                pl.semaphore_wait(barrier, len(met))
-                met_all = True
+            if c:
+                gather(r * block + c * part, part)
             query_copy(r, c).start()
     gather(0, block)
 
@@ -324,14 +325,13 @@
         total.append(here)
     late = (row // layers) % STEPS == 1
     squares[0] = jnp.where(late, total[1], total[0])
-    sends = []
-    for k, device in enumerate(others):
+    for other in others:
         copy = pltpu.make_async_remote_copy(
             src_ref=squares.at[0],
-            dst_ref=squares.at[k + 1],
+            dst_ref=squares.at[(other - shard) & (shards - 1)],
             send_sem=square_send,
             recv_sem=square_recv,
-            device_id=device,
+            device_id=(group, other),
             device_id_type=MESH,
         )
         copy.start()

time: 28.9 us -> 28.9 us (level)
  no operation moved by 1% of the time
where the time goes in v5:
time: 28.9 us; the launch traced here: 28.8 us
  Pallas kernels  27.8 us (96%)
  local copies, waits for them, and re-layouts  0.97 us (3%)
    pallas_call x1, Pallas kernels, local(): pl.pallas_call(functools.partial(kernel, groups, shards), out_shape=jax.S...  27.8 us
    unnamed x1, local copies, waits for them, and re-layouts  0.97 us

profile of v5, /device:TPU:128, one launch (start us, length us, event | category | flops | bytes accessed | tf_op | source)
XLA Modules:
  0.0 28.8 jit_solution(14291135299904458322)
XLA Ops:
  0.0 27.8 %shard_map.91 = f32[128,16,128]{2,1,0:T(8,128)S(1)} custom-call(bf16[8,2,4,128,128]{4,3,2,1,0:T(8,128)(2,1)} %states_hbm.1, s32[1,256]{1,0:T(1,128)} %bitcast.38, s32[1,128]{1,0:T(1,128)} %bitcast.39, bf16[128,16,128]{2,1,0:T(8,128)(2,1)} %bitcast.33, bf16[128,16,128]{2,1,0:T(8,128)(2,1)} %bitcast.34, bf16[128,16,128]{2,1,0:T(8,128)(2,1)} %bitcast.35, ...), custom_call_target="tpu_custom_call" | custom-call | flops 67108864 | bytes 5242880 | tf_op jit(solution)/shard_map/pallas_call | solution.py:382
  27.8 1.0 %copy.17 = f32[128,2,2,512]{3,2,1,0:T(2,128)} copy(f32[128,2,2,512]{3,2,1,0:T(2,128)S(1)} %bitcast.32) | data formatting | bytes 2097152
